TPU v7x, 128 devices: a whole 4x4x4 slice. The times are simulated.
128 devices in a mesh: grp: 4 (over z_lo, core), blk: 32 (over x, y, z_hi).
Axes of the slice: x: 4, y: 4, z: 4 (z_hi: 2, z_lo: 2; z = z_hi * 2 + z_lo), core: 2. Of those that a mesh axis runs over, the one named last changes fastest.
Arguments:
- embeddings: bfloat16 [98304, 512], P(('grp', 'blk')), may hold values from -6 to 6
- cluster_ids: int32 [98304], P(('grp', 'blk')), may hold values from 0 to 11, as said below
Outputs:
- best: float32 [98304], P(('grp', 'blk'))
- cluster_mean: float32 [12], replicated
Inputs may be any that keep to these rules, and one draw needn't show every extreme that they name: `cluster_ids`: items of one cluster are contiguous and lie within one block of 24576 items (group g holds clusters 3 * g to 3 * g + 2, each non-empty with 3072 items or more); ids never fall along the items.
All inputs are finite; a program needn't handle non-finite values.
Results may differ from a plain program's by a relative error of at most 0.0012.
Values may be sent and summed in bfloat16 or wider, within the bound.
A program may use at most 64 MiB of HBM per device.

v0:
```python
import jax
import jax.numpy as jnp
from jax import lax
from jax.sharding import PartitionSpec as P

CL_GRP = 3


def tile_max(unit, own_ids, own_pos, piece_units, piece_ids, start):
    scores = lax.dot_general(
        unit, piece_units, (((1,), (1,)), ((), ())), preferred_element_type=jnp.float32
    )
    columns = start + jnp.arange(piece_units.shape[0], dtype=jnp.int32)
    same = (own_ids[:, None] == piece_ids.astype(jnp.float32)[None, :]) & (
        own_pos[:, None] != columns[None, :]
    )
    masked = jnp.where(same, scores, jnp.float32(-4.0))
    return (jnp.max(masked, axis=1), jnp.max(masked, axis=0))


def per_device(embeddings, cluster_ids):
    rows = embeddings.shape[0]
    width = embeddings.shape[1]
    wide = embeddings.astype(jnp.float32)
    norms = jnp.sum(wide * wide, axis=1)
    unit = (wide * lax.rsqrt(norms + 1e-06)[:, None]).astype(jnp.bfloat16)
    own_ids = cluster_ids.astype(jnp.float32)
    ids_narrow = cluster_ids.astype(jnp.bfloat16)
    my_index = lax.axis_index("blk")
    own_pos = my_index * rows + jnp.arange(rows, dtype=jnp.int32)
    floor_value = jnp.full((rows,), -4.0, jnp.float32)
    piece_units = lax.all_gather(unit, "blk", axis=0, tiled=True)
    piece_ids = lax.all_gather(ids_narrow, "blk", axis=0, tiled=True)
    length = piece_units.shape[0]
    count = length // rows
    unit_blocks = piece_units.reshape(count, rows, width)
    id_blocks = piece_ids.reshape(count, rows)

    def inner(current, item):
        block_units, block_ids, number = item
        row_max, column_max = tile_max(
            unit, own_ids, own_pos, block_units, block_ids, number * rows
        )
        return (jnp.maximum(current, row_max), None)

    result, unused = lax.scan(
        inner, floor_value, (unit_blocks, id_blocks, jnp.arange(count, dtype=jnp.int32))
    )
    clusters = CL_GRP * lax.axis_size("grp")
    onehot = (cluster_ids[:, None] == jnp.arange(clusters, dtype=jnp.int32)[None, :]).astype(
        jnp.float32
    )
    sums = jnp.dot(
        result, onehot, precision=lax.Precision.HIGHEST, preferred_element_type=jnp.float32
    )
    counts = jnp.sum(onehot, axis=0)
    total_sums, total_counts = lax.psum((sums, counts), ("grp", "blk"))
    return (result, total_sums / total_counts)


def solution(mesh):
    placed = (P(("grp", "blk"), None), P(("grp", "blk")))
    return jax.shard_map(
        per_device, mesh=mesh, in_specs=placed, out_specs=(P(("grp", "blk")), P()), check_vma=False
    )
```

profile of v0, /device:TPU:1, one launch (start us, length us, event | category | flops | bytes accessed | tf_op | source)
XLA Modules:
  0.0 410.2 jit_solution(16947668866230390850)
XLA Ops:
  8.6 2.3 fusion.7
  11.0 83.9 %all-gather = bf16[32,1,768]{2,1,0:T(2,128)(2,1)S(1)} all-gather(bf16[1,1,768]{2,1,0:T(2,128)(2,1)S(1)} %reshape.26), channel_id=1, replica_groups=mesh['grp'=4,'blk'=32] {'blk'}, dimensions={0}, use_global_device_ids=true | all-gather | bytes 50688 | tf_op jit(solution)/shard_map/all_gather | solution.py:33
  95.0 128.5 %all-gather.3.cloned.1.call-done = bf16[24576,512]{1,0:T(8,128)(2,1)} async-done(((bf16[768,512]{1,0:T(8,128)(2,1)}), bf16[24576,512]{1,0:T(8,128)(2,1)}) %all-gather.3.cloned.1.call-update) | async-done | bytes 25165840 | tf_op jit(solution)/shard_map/all_gather | solution.py:32
  223.5 114.6 %while.11 = (s32[]{:T(128)}, f32[768]{0:T(1024)S(1)}, f32[768]{0:T(1024)S(1)}, bf16[32,768]{1,0:T(8,128)(2,1)S(1)}, s32[32]{0:T(128)S(1)}, /*index=5*/bf16[32,76...) while((s32[]{:T(128)}, f32[768]{0:T(1024)S(1)}, ...), condition=%wide.region_3.4_spmd.clone, body=%wide.region_1.3_spmd.clone.sunk | while | flops 606931968 | bytes 1608359 | solution.py:46
  228.3 2.3 fusion.17
  231.9 2.3 fusion.17
  235.5 2.3 fusion.17
  239.1 2.3 fusion.17
  242.7 2.3 fusion.17
  246.2 2.3 fusion.17
  249.8 2.3 fusion.17
  253.4 2.3 fusion.17
  257.0 2.3 fusion.17
  260.6 2.3 fusion.17
  264.2 2.3 fusion.17
  274.9 2.3 fusion.17
  282.1 2.3 fusion.17
  289.2 2.3 fusion.17
  296.4 2.3 fusion.17
  303.5 2.3 fusion.17
  317.9 2.3 fusion.17
  325.0 2.3 fusion.17
  332.2 2.3 fusion.17
  338.2 64.7 %all-reduce = (f32[12]{0:T(128)S(1)}, f32[12]{0:T(128)S(1)}) all-reduce(f32[12]{0:T(128)S(1)} %convolution_bitcast_fusion, f32[12]{0:T(128)S(1)} %convert_reduce_fusion.1), channel_id=1, replica_groups=mesh['grp'=4,'blk'=32] {'grp','blk'}, use_global_device_ids=true, to_apply=%region_4.5 | all-reduce | flops 24 | bytes 192 | tf_op jit(solution)/shard_map/psum | solution.py:57
  (158 shorter events, 52.5 us)
Async XLA Ops:
  7.2 3.8 copy-start.1
  7.2 216.3 %all-gather.3.cloned.1.call-start = ((), (), s32[]{:S(2)}) async-start(), calls=%async_computation | async-start | bytes 25952256 | tf_op jit(solution)/shard_map/all_gather | solution.py:32
  338.0 65.3 %copy-start = (f32[768]{0:T(1024)}, f32[768]{0:T(1024)S(1)}, u32[]{:S(2)}) copy-start(f32[768]{0:T(1024)S(1)} %get-tuple-element.42) | copy-start | bytes 9220
Sparse Core Ops, SparseCore 0:
  11.0 212.3 all-gather.2
where the time goes:
time: 412 us; the launch traced here: 410 us
  blocking collectives  149 us (36%)
  waiting for transfers between devices  128 us (31%)
  matrix products  72.6 us (18%)
  loops' own time  21.2 us (5%)
  local copies, waits for them, and re-layouts  19.9 us (5%)
  between operations  14.1 us (3%)
  other arithmetic  5.4 us (1%)
    all_gather x1, waiting for transfers between devices, per_device(): piece_units = lax.all_gather(unit, 'blk', axis=0, tiled=True)  128 us
    all_gather x1, blocking collectives, per_device(): piece_ids = lax.all_gather(ids_narrow, 'blk', axis=0, tiled=True)  83.9 us
    dot_general x32, matrix products, tile_max(): lax.dot_general(unit, piece_units, (((1,), (1,)), ((), ())), preferred_el...  72.4 us
    psum x1, blocking collectives, per_device(): total_sums, total_counts = lax.psum((sums, counts), ('grp', 'blk'))  64.7 us
    another operation x1, loops' own time, per_device(): lax.scan(inner, floor_value, (unit_blocks, id_blocks, jnp.arange(count, d...  21.2 us
    dynamic_slice x32, local copies, waits for them, and re-layouts, per_device(): lax.scan(inner, floor_value, (unit_blocks, id_blocks, jnp.arange(count, d...  19.8 us
  transfers between devices with their start and end apart: 1, of which 1 were waited for; matrix products, arithmetic and copies ran while one was open for 0% of the time, Pallas kernels for 0%

commit v1 on v0

v1 whole, which is shorter than its diff:
```python
import functools

import jax
import jax.numpy as jnp
from jax import lax
from jax.experimental import pallas as pl
from jax.experimental.pallas import tpu as pltpu
from jax.sharding import PartitionSpec as P

MESH = pl.DeviceIdType.MESH
CL_GRP = 3
FLOOR = -4.0
PIECE = 128
TILE = 256

OWN, B, C, F, G, A, E, RELAY = range(8)
HELD = {B: (1, 0, 0), C: (1, 1, 0), F: (0, 3, 1), G: (3, 0, 1), A: (3, 0, 0), E: (1, 2, 0)}
LINKS = {
    A: (OWN, (1, 0, 0)),
    B: (OWN, (3, 0, 0)),
    C: (B, (0, 3, 0)),
    E: (C, (0, 3, 0)),
    RELAY: (OWN, (0, 0, 1)),
    F: (RELAY, (0, 1, 0)),
    G: (RELAY, (1, 0, 0)),
}
WHOLE = ((B, OWN), (C, OWN), (C, B), (A, C), (F, OWN), (F, B), (F, C), (G, OWN), (G, B), (G, C), (G, F), (E, OWN))
HALVED = ((A, B), (F, A), (G, A), (E, B), (E, F), (E, G), (E, A))
PASS, SEND, TILE_OF = range(3)
ORDER = (
    (TILE_OF, OWN, 0), (TILE_OF, OWN, 1), (TILE_OF, OWN, 2),
    (PASS, B, 0), (PASS, RELAY, 0), (PASS, B, 1), (PASS, B, 2), (TILE_OF, B, 0), (PASS, RELAY, 1), (PASS, C, 0),
    (PASS, B, 3), (TILE_OF, B, 1), (PASS, C, 1), (PASS, RELAY, 2), (TILE_OF, A, 0), (PASS, B, 4), (PASS, C, 2),
    (TILE_OF, F, 0), (TILE_OF, G, 0), (PASS, RELAY, 3), (TILE_OF, C, 0), (PASS, B, 5), (PASS, C, 3), (TILE_OF, B, 2),
    (PASS, RELAY, 4), (SEND, A, 3), (PASS, C, 4), (TILE_OF, C, 1), (TILE_OF, F, 1), (TILE_OF, G, 1), (PASS, RELAY, 5),
    (SEND, A, 4), (SEND, A, 5), (PASS, C, 5), (TILE_OF, E, 0), (TILE_OF, C, 2), (TILE_OF, E, 1), (TILE_OF, F, 2),
    (TILE_OF, G, 2), (TILE_OF, A, 1), (TILE_OF, A, 2), (TILE_OF, E, 2),
)


def kernel(x_hbm, ids_hbm, best_ref, mean_ref, x_ref, ids_ref, held, row_max, col_max, row_ids, col_ids, counts, back, got,
           sums, total, x_sem, send_sem, recv_sem, ids_send, ids_recv, back_send, back_recv, sum_send, sum_recv, tot_send,
           tot_recv):
    rows, width = x_ref.shape
    pieces, tiles = rows // PIECE, rows // TILE
    grp, blk = lax.axis_index("grp"), lax.axis_index("blk")
    x, y, z = blk // 8, (blk // 2) % 4, blk % 2
    swap = (z + grp) % 2

    def load(q):
        window = pl.ds(q * PIECE, PIECE)
        return pltpu.make_async_copy(x_hbm.at[window], x_ref.at[window], x_sem.at[q])

    load_ids = pltpu.make_async_copy(ids_hbm, ids_ref, x_sem.at[pieces])
    load_ids.start()
    for q in range(pieces):
        load(q).start()

    def place(nx, ny, nz):
        return (lax.rem(nx + 8, 4) * 4 + lax.rem(ny + 8, 4)) * 2 + lax.rem(nz, 2)

    def times(step):
        dx, dy, dz = step
        return (grp, place(x + dx * (1 - swap) + dy * swap, y + dy * (1 - swap) + dx * swap, z + dz))

    plane = [(dx, dy) for dx in range(4) for dy in range(4) if dx or dy]
    across = [(dz, dg) for dz in range(2) for dg in range(4) if dz or dg]

    def in_plane(dx, dy):
        return (grp, place(x + dx, y + dy, z))

    def over(dz, dg):
        return (lax.rem(grp + dg, 4), place(x, y, z + dz))

    barrier = pltpu.get_barrier_semaphore()
    greeted = [in_plane(*p) for p in ((0, 1), (0, 3), (1, 0), (3, 0))] + [over(*a) for a in across]
    for device in greeted:
        pl.semaphore_signal(barrier, inc=1, device_id=device, device_id_type=MESH)

    def copy(slot, q):
        source, step = LINKS[slot]
        window = pl.ds(q * PIECE, PIECE)
        return pltpu.make_async_remote_copy(
            src_ref=held.at[source, window], dst_ref=held.at[slot, window], send_sem=send_sem.at[slot - 1, q],
            recv_sem=recv_sem.at[slot - 1, q], device_id=times(step), device_id_type=MESH)

    def ids_copy(slot):
        source, step = LINKS[slot]
        return pltpu.make_async_remote_copy(
            src_ref=counts.at[source], dst_ref=counts.at[slot], send_sem=ids_send.at[slot - 1],
            recv_sem=ids_recv.at[slot - 1], device_id=times(step), device_id_type=MESH)

    def back_copy(slot):
        return pltpu.make_async_remote_copy(
            src_ref=back.at[slot], dst_ref=got.at[slot], send_sem=back_send.at[slot - 1],
            recv_sem=back_recv.at[slot - 1], device_id=times(HELD[slot]), device_id_type=MESH)

    def normalise(q):
        load(q).wait()
        window = pl.ds(q * PIECE, PIECE)
        wide = x_ref[window, :].astype(jnp.float32)
        norms = jnp.sum(wide * wide, axis=1, keepdims=True)
        held[OWN, window, :] = (wide * lax.rsqrt(norms + 1e-06)).astype(jnp.bfloat16)

    def fill_ids(slot):
        low, high = counts[slot, 0:1, :], counts[slot, 1:2, :]
        at = lax.broadcasted_iota(jnp.int32, (rows, 128), 0).astype(jnp.float32)
        row_ids[slot] = (at >= low).astype(jnp.float32) + (at >= high).astype(jnp.float32)
        for j in range(rows // 128):
            at = (lax.broadcasted_iota(jnp.int32, (8, 128), 1) + 128 * j).astype(jnp.float32)
            col_ids[slot, :, pl.ds(128 * j, 128)] = (at >= low).astype(jnp.float32) + (at >= high).astype(jnp.float32)

    def product(j, first, n, s, q, diagonal=False):
        window = pl.ds(q * TILE, TILE)
        scores = lax.dot_general(held[j, pl.ds(first, n), :], held[s, window, :], (((1,), (1,)), ((), ())),
                                 preferred_element_type=jnp.float32)
        ids = row_ids[j, pl.ds(first, n), :]
        same = jnp.concatenate([ids] * (TILE // 128), axis=1) == col_ids[s, 0:1, window]
        if diagonal:
            same = same & (lax.broadcasted_iota(jnp.int32, (n, TILE), 0) != lax.broadcasted_iota(jnp.int32, (n, TILE), 1))
        masked = jnp.where(same, scores, jnp.float32(FLOOR))
        across_tile = functools.reduce(jnp.maximum, [masked[:, 128 * t:128 * t + 128] for t in range(TILE // 128)])
        row_max[j, pl.ds(first, n), :] = jnp.maximum(row_max[j, pl.ds(first, n), :], across_tile)
        if not diagonal:
            down = jnp.max(masked.reshape(n // 8, 8, TILE), axis=0)
            col_max[s, :, window] = jnp.maximum(col_max[s, :, window], down)

    waited, ready, tiles_in = set(), set(), set()

    def wait(slot, q):
        if (slot, q) not in waited:
            waited.add((slot, q))
            copy(slot, q).wait_recv()

    def wait_ids(slot):
        if slot not in ready:
            ready.add(slot)
            ids_copy(slot).wait_recv()
            if slot != RELAY:
                fill_ids(slot)

    def wanted(s, q, j, r):
        if (s, j) in WHOLE or (j, s) in WHOLE:
            return True
        return ((s, j) in HALVED and r >= q) or ((j, s) in HALVED and q >= r)

    def multiply(s, q):
        tiles_in.add((s, q))
        if s == OWN:
            product(OWN, q * TILE, TILE, OWN, q, diagonal=True)
            if q + 1 < tiles:
                product(OWN, (q + 1) * TILE, rows - (q + 1) * TILE, OWN, q)
            return
        for p in range(q * TILE // PIECE, (q + 1) * TILE // PIECE):
            wait(s, p)
        wait_ids(s)
        for j in (OWN, *HELD):
            if j == s:
                continue
            r = 0
            while r < tiles:
                end = r
                while end < tiles and (j, end) in tiles_in and wanted(s, q, j, end):
                    end += 1
                if end > r:
                    product(j, r * TILE, (end - r) * TILE, s, q)
                r = end + 1

    def pass_on(slot, q):
        wait(slot, q)
        onward = [to for to, (source, _) in LINKS.items() if source == slot]
        for to in onward:
            copy(to, q).start()
        if q == 0:
            wait_ids(slot)
            for to in onward:
                ids_copy(to).start()

    load_ids.wait()
    ids = ids_ref[...].reshape(1, rows)
    base = grp * CL_GRP
    low = jnp.sum((ids <= base).astype(jnp.float32), axis=1, keepdims=True)
    high = jnp.sum((ids <= base + 1).astype(jnp.float32), axis=1, keepdims=True)
    counts[OWN] = jnp.where(lax.broadcasted_iota(jnp.int32, (8, 128), 0) == 0, low, high)

    normalise(0)
    pl.semaphore_wait(barrier, len(greeted))
    early = [q for q in range(pieces) if (SEND, A, q) not in ORDER]
    for q in range(pieces):
        if q:
            normalise(q)
        for slot in (B, RELAY, A):
            if slot != A or q in early:
                copy(slot, q).start()
            if q == 0:
                ids_copy(slot).start()
    fill_ids(OWN)
    row_max[...] = jnp.full_like(row_max, FLOOR)
    col_max[...] = jnp.full_like(col_max, FLOOR)

    for action, slot, q in ORDER:
        if action == PASS:
            pass_on(slot, q)
        elif action == SEND:
            copy(slot, q).start()
        else:
            multiply(slot, q)

    def finish(slot):
        for j in range(rows // 128):
            window = pl.ds(128 * j, 128)
            across_rows = jnp.max(row_max[slot, window, :].T, axis=0, keepdims=True)
            back[slot, :, window] = jnp.maximum(across_rows, jnp.max(col_max[slot, :, window], axis=0, keepdims=True))

    for slot in HELD:
        finish(slot)
        back_copy(slot).start()
    finish(OWN)
    best = back[OWN]
    for slot in HELD:
        back_copy(slot).wait_recv()
        best = jnp.maximum(best, got[slot])
    best_ref[...] = best.reshape(rows)

    own = col_ids[OWN, 0:1, :]
    lane = lax.broadcasted_iota(jnp.int32, (1, 128), 1)
    partial = jnp.zeros((1, 128), jnp.float32)
    for c in range(CL_GRP):
        member = own == jnp.float32(c)
        amount = jnp.sum(jnp.where(member, best, 0.0), axis=1, keepdims=True)
        number = jnp.sum(member.astype(jnp.float32), axis=1, keepdims=True)
        partial = partial + jnp.where(lane == base + c, amount, 0.0) + jnp.where(lane == base + c + 64, number, 0.0)

    def exchange(buffer, value, me, partners, send, recv):
        buffer[me] = value
        copies = []
        for i, device in enumerate(partners):
            copies.append(pltpu.make_async_remote_copy(
                src_ref=buffer.at[me], dst_ref=buffer.at[me], send_sem=send.at[i], recv_sem=recv.at[i],
                device_id=device, device_id_type=MESH))
            copies[-1].start()
        for c in copies:
            c.wait_recv()
        return functools.reduce(jnp.add, [buffer[i] for i in range(len(partners) + 1)]), copies

    part, first = exchange(sums, partial, x * 4 + y, [in_plane(*p) for p in plane], sum_send, sum_recv)
    whole, second = exchange(total, part, z * 4 + grp, [over(*a) for a in across], tot_send, tot_recv)
    mean = whole / jnp.concatenate([whole[:, 64:], whole[:, :64]], axis=1)
    mean_ref[...] = mean.reshape(128)[:mean_ref.shape[0]]

    for slot in LINKS:
        for q in range(pieces):
            copy(slot, q).wait_send()
        ids_copy(slot).wait_send()
    for slot in HELD:
        back_copy(slot).wait_send()
    for c in first + second:
        c.wait_send()


def per_device(embeddings, cluster_ids):
    rows, width = embeddings.shape
    pieces = rows // PIECE
    dma = pltpu.SemaphoreType.DMA
    hbm = pl.BlockSpec(memory_space=pltpu.HBM)
    vmem = pl.BlockSpec(memory_space=pltpu.VMEM)
    return pl.pallas_call(
        kernel,
        out_shape=(jax.ShapeDtypeStruct((rows,), jnp.float32),
                   jax.ShapeDtypeStruct((CL_GRP * lax.axis_size("grp"),), jnp.float32)),
        in_specs=[hbm, hbm],
        out_specs=(vmem, vmem),
        scratch_shapes=[
            pltpu.VMEM((rows, width), jnp.bfloat16),
            pltpu.VMEM((rows,), jnp.int32),
            pltpu.VMEM((8, rows, width), jnp.bfloat16),
            pltpu.VMEM((7, rows, 128), jnp.float32),
            pltpu.VMEM((7, 8, rows), jnp.float32),
            pltpu.VMEM((7, rows, 128), jnp.float32),
            pltpu.VMEM((7, 8, rows), jnp.float32),
            pltpu.VMEM((8, 8, 128), jnp.float32),
            pltpu.VMEM((7, 1, rows), jnp.float32),
            pltpu.VMEM((7, 1, rows), jnp.float32),
            pltpu.VMEM((16, 1, 128), jnp.float32),
            pltpu.VMEM((8, 1, 128), jnp.float32),
            dma((pieces + 1,)),
            dma((7, pieces)), dma((7, pieces)),
            dma((7,)), dma((7,)),
            dma((6,)), dma((6,)),
            dma((15,)), dma((15,)),
            dma((7,)), dma((7,)),
        ],
        compiler_params=pltpu.CompilerParams(collective_id=0, has_side_effects=True, vmem_limit_bytes=63 * 2**20),
    )(embeddings, cluster_ids)


def solution(mesh):
    placed = (P(("grp", "blk"), None), P(("grp", "blk")))
    return jax.shard_map(
        per_device, mesh=mesh, in_specs=placed, out_specs=(P(("grp", "blk")), P()), check_vma=False
    )
```

time: 412 us -> 59.7 us (0.14)
  blocking collectives: 149 us -> 0 us
  waiting for transfers between devices: 128 us -> 0 us
  matrix products: 72.6 us -> 0 us
  Pallas kernels: 0 us -> 57.1 us
  loops' own time: 21.2 us -> 0 us
  local copies, waits for them, and re-layouts: 19.9 us -> 1.78 us
  between operations: 14.1 us -> 0.65 us
  other arithmetic: 5.4 us -> 0 us
    all_gather x1 -> x0, waiting for transfers between devices: 128 us -> none  [per_device(): piece_units = lax.all_gather(unit, 'blk', axis=0, tiled=True)]
    all_gather x1 -> x0, blocking collectives: 83.9 us -> none  [per_device(): piece_ids = lax.all_gather(ids_narrow, 'blk', axis=0, tiled=True)]
    dot_general x33 -> x0, matrix products: 72.6 us -> none  [the longest x32 72.4 us: tile_max(): lax.dot_general(unit, piece_units, (((1,), (1,)), ((), ())), preferred_el...]
    psum x1 -> x0, blocking collectives: 64.7 us -> none  [per_device(): total_sums, total_counts = lax.psum((sums, counts), ('grp', 'blk'))]
    pallas_call x0 -> x1, Pallas kernels: none -> 57.1 us  [per_device(): pl.pallas_call(kernel, out_shape=(jax.ShapeDtypeStruct((rows,), jnp.float...]
    another operation x1 -> x0, loops' own time: 21.2 us -> none  [per_device(): lax.scan(inner, floor_value, (unit_blocks, id_blocks, jnp.arange(count, d...]
    dynamic_slice x32 -> x0, local copies, waits for them, and re-layouts: 19.8 us -> none  [per_device(): lax.scan(inner, floor_value, (unit_blocks, id_blocks, jnp.arange(count, d...]
  transfers between devices with their start and end apart: 1 -> 0, of which waited for: 1 -> 0; matrix products, arithmetic and copies ran while one was open for 0% -> 0% of each run, Pallas kernels for 0% -> 0%
where the time goes in v1:
time: 59.7 us; the launch traced here: 59.5 us
  Pallas kernels  57.1 us (96%)
  local copies, waits for them, and re-layouts  1.78 us (3%)
  between operations  0.65 us (1%)
    pallas_call x1, Pallas kernels, per_device(): pl.pallas_call(kernel, out_shape=(jax.ShapeDtypeStruct((rows,), jnp.float...  57.1 us
    unnamed x4, local copies, waits for them, and re-layouts  1.78 us

profile of v1, /device:TPU:1, one launch (start us, length us, event | category | flops | bytes accessed | tf_op | source)
XLA Modules:
  0.0 59.5 jit_solution(4539852114065234971)
XLA Ops:
  0.6 57.1 %shard_map.41 = (f32[768]{0:T(1024)}, f32[12]{0:T(128)}) custom-call(bf16[768,512]{1,0:T(8,128)(2,1)} %x_hbm.1, s32[768]{0:T(1024)} %ids_hbm.1), custom_call_target="tpu_custom_call" | custom-call | tf_op jit(solution)/shard_map/pallas_call | solution.py:267
  57.7 0.0 copy-start
  57.8 1.3 %copy.6 = f32[768]{0:T(1024)} copy(f32[768]{0:T(1024)} %get-tuple-element.4) | data formatting | bytes 6144
  59.0 0.0 copy-done
  59.0 0.5 copy.7
Async XLA Ops:
  57.7 1.3 %copy-start = (f32[12]{0:T(128)S(1)}, f32[12]{0:T(128)}, u32[]{:S(2)}) copy-start(f32[12]{0:T(128)} %get-tuple-element.5) | copy-start | bytes 148

commit v2 on v1

--- a/solution.py
+++ b/solution.py
@@ -25,22 +25,53 @@
     G: (RELAY, (1, 0, 0)),
 }
 WHOLE = ((B, OWN), (C, OWN), (C, B), (A, C), (F, OWN), (F, B), (F, C), (G, OWN), (G, B), (G, C), (G, F), (E, OWN))
-HALVED = ((A, B), (F, A), (G, A), (E, B), (E, F), (E, G), (E, A))
+HALVED = ((A, B), (A, F), (A, G), (E, B), (E, F), (E, G), (E, A))
 PASS, SEND, TILE_OF = range(3)
 ORDER = (
-    (TILE_OF, OWN, 0), (TILE_OF, OWN, 1), (TILE_OF, OWN, 2),
-    (PASS, B, 0), (PASS, RELAY, 0), (PASS, B, 1), (PASS, B, 2), (TILE_OF, B, 0), (PASS, RELAY, 1), (PASS, C, 0),
-    (PASS, B, 3), (TILE_OF, B, 1), (PASS, C, 1), (PASS, RELAY, 2), (TILE_OF, A, 0), (PASS, B, 4), (PASS, C, 2),
-    (TILE_OF, F, 0), (TILE_OF, G, 0), (PASS, RELAY, 3), (TILE_OF, C, 0), (PASS, B, 5), (PASS, C, 3), (TILE_OF, B, 2),
-    (PASS, RELAY, 4), (SEND, A, 3), (PASS, C, 4), (TILE_OF, C, 1), (TILE_OF, F, 1), (TILE_OF, G, 1), (PASS, RELAY, 5),
-    (SEND, A, 4), (SEND, A, 5), (PASS, C, 5), (TILE_OF, E, 0), (TILE_OF, C, 2), (TILE_OF, E, 1), (TILE_OF, F, 2),
-    (TILE_OF, G, 2), (TILE_OF, A, 1), (TILE_OF, A, 2), (TILE_OF, E, 2),
+    (PASS, B, 0),
+    (PASS, B, 1),
+    (TILE_OF, A, 0),
+    (TILE_OF, B, 0),
+    (PASS, RELAY, 0),
+    (PASS, B, 2),
+    (TILE_OF, A, 1),
+    (PASS, RELAY, 1),
+    (PASS, B, 3),
+    (PASS, C, 0),
+    (TILE_OF, B, 1),
+    (PASS, RELAY, 2),
+    (PASS, C, 1),
+    (TILE_OF, C, 0),
+    (PASS, B, 4),
+    (TILE_OF, G, 0),
+    (PASS, RELAY, 3),
+    (TILE_OF, F, 0),
+    (PASS, C, 2),
+    (PASS, B, 5),
+    (PASS, RELAY, 4),
+    (TILE_OF, B, 2),
+    (PASS, C, 3),
+    (TILE_OF, C, 1),
+    (PASS, RELAY, 5),
+    (SEND, A, 4),
+    (SEND, A, 5),
+    (TILE_OF, E, 0),
+    (TILE_OF, G, 1),
+    (PASS, C, 4),
+    (TILE_OF, F, 1),
+    (PASS, C, 5),
+    (TILE_OF, C, 2),
+    (TILE_OF, E, 1),
+    (TILE_OF, F, 2),
+    (TILE_OF, G, 2),
+    (TILE_OF, A, 2),
+    (TILE_OF, E, 2),
 )
 
 
 def kernel(x_hbm, ids_hbm, best_ref, mean_ref, x_ref, ids_ref, held, row_max, col_max, row_ids, col_ids, counts, back, got,
            sums, total, x_sem, send_sem, recv_sem, ids_send, ids_recv, back_send, back_recv, sum_send, sum_recv, tot_send,
-           tot_recv):
+           tot_recv, arrived):
     rows, width = x_ref.shape
     pieces, tiles = rows // PIECE, rows // TILE
     grp, blk = lax.axis_index("grp"), lax.axis_index("blk")
@@ -52,9 +83,9 @@
         return pltpu.make_async_copy(x_hbm.at[window], x_ref.at[window], x_sem.at[q])
 
     load_ids = pltpu.make_async_copy(ids_hbm, ids_ref, x_sem.at[pieces])
-    load_ids.start()
     for q in range(pieces):
         load(q).start()
+    load_ids.start()
 
     def place(nx, ny, nz):
         return (lax.rem(nx + 8, 4) * 4 + lax.rem(ny + 8, 4)) * 2 + lax.rem(nz, 2)
@@ -63,17 +94,19 @@
         dx, dy, dz = step
         return (grp, place(x + dx * (1 - swap) + dy * swap, y + dy * (1 - swap) + dx * swap, z + dz))
 
-    plane = [(dx, dy) for dx in range(4) for dy in range(4) if dx or dy]
-    across = [(dz, dg) for dz in range(2) for dg in range(4) if dz or dg]
-
     def in_plane(dx, dy):
         return (grp, place(x + dx, y + dy, z))
 
-    def over(dz, dg):
-        return (lax.rem(grp + dg, 4), place(x, y, z + dz))
+    def over(dz, dl, dc):
+        return (lax.rem(grp // 2 + dl, 2) * 2 + lax.rem(grp + dc, 2), place(x, y, z + dz))
+
+    plane = [(dx, dy) for dx in range(4) for dy in range(4) if dx or dy]
+    plane.sort(key=lambda p: -sum(min(d, 4 - d) for d in p))
+    same_core = [(1, 0, 0), (0, 1, 0), (1, 1, 0)]
+    other_core = [(1, 0, 1), (0, 1, 1), (1, 1, 1), (0, 0, 1)]
 
     barrier = pltpu.get_barrier_semaphore()
-    greeted = [in_plane(*p) for p in ((0, 1), (0, 3), (1, 0), (3, 0))] + [over(*a) for a in across]
+    greeted = [over(*a) for a in same_core] + [in_plane(*p) for p in ((0, 1), (0, 3), (1, 0), (3, 0))] + [over(0, 0, 1)]
     for device in greeted:
         pl.semaphore_signal(barrier, inc=1, device_id=device, device_id_type=MESH)
 
@@ -183,20 +216,31 @@
     high = jnp.sum((ids <= base + 1).astype(jnp.float32), axis=1, keepdims=True)
     counts[OWN] = jnp.where(lax.broadcasted_iota(jnp.int32, (8, 128), 0) == 0, low, high)
 
-    normalise(0)
+    for q in range(pieces):
+        normalise(q)
+    fill_ids(OWN)
+    row_max[...] = jnp.full_like(row_max, FLOOR)
+    col_max[...] = jnp.full_like(col_max, FLOOR)
+    for q in range(tiles):
+        multiply(OWN, q)
+
     pl.semaphore_wait(barrier, len(greeted))
     early = [q for q in range(pieces) if (SEND, A, q) not in ORDER]
     for q in range(pieces):
-        if q:
-            normalise(q)
         for slot in (B, RELAY, A):
             if slot != A or q in early:
                 copy(slot, q).start()
             if q == 0:
                 ids_copy(slot).start()
-    fill_ids(OWN)
-    row_max[...] = jnp.full_like(row_max, FLOOR)
-    col_max[...] = jnp.full_like(col_max, FLOOR)
+    for a in same_core:
+        pl.semaphore_signal(arrived, inc=1, device_id=over(*a), device_id_type=MESH)
+    relative = col_ids[OWN, 0:1, :]
+    sublane = lax.broadcasted_iota(jnp.int32, (8, 1), 0)
+    lane = lax.broadcasted_iota(jnp.int32, (8, 128), 1)
+    member = relative == sublane.astype(jnp.float32)
+    number = jnp.sum(member.astype(jnp.float32), axis=1, keepdims=True)
+    here = lane == base + sublane
+    numbers = jnp.sum(jnp.where((lane == base + sublane + 64) & (sublane < CL_GRP), number, 0.0), axis=0, keepdims=True)
 
     for action, slot, q in ORDER:
         if action == PASS:
@@ -212,24 +256,22 @@
             across_rows = jnp.max(row_max[slot, window, :].T, axis=0, keepdims=True)
             back[slot, :, window] = jnp.maximum(across_rows, jnp.max(col_max[slot, :, window], axis=0, keepdims=True))
 
-    for slot in HELD:
+    for slot in (E, F, G, C, A, B):
         finish(slot)
         back_copy(slot).start()
     finish(OWN)
+    for slot in LINKS:
+        for q in range(pieces):
+            copy(slot, q).wait_send()
+        ids_copy(slot).wait_send()
+    pl.semaphore_wait(arrived, len(same_core))
     best = back[OWN]
     for slot in HELD:
         back_copy(slot).wait_recv()
         best = jnp.maximum(best, got[slot])
-    best_ref[...] = best.reshape(rows)
-
-    own = col_ids[OWN, 0:1, :]
-    lane = lax.broadcasted_iota(jnp.int32, (1, 128), 1)
-    partial = jnp.zeros((1, 128), jnp.float32)
-    for c in range(CL_GRP):
-        member = own == jnp.float32(c)
-        amount = jnp.sum(jnp.where(member, best, 0.0), axis=1, keepdims=True)
-        number = jnp.sum(member.astype(jnp.float32), axis=1, keepdims=True)
-        partial = partial + jnp.where(lane == base + c, amount, 0.0) + jnp.where(lane == base + c + 64, number, 0.0)
+
+    amount = jnp.sum(jnp.where(member, best, 0.0), axis=1, keepdims=True)
+    partial = numbers + jnp.sum(jnp.where(here & (sublane < CL_GRP), amount, 0.0), axis=0, keepdims=True)
 
     def exchange(buffer, value, me, partners, send, recv):
         buffer[me] = value
@@ -239,22 +281,25 @@
                 src_ref=buffer.at[me], dst_ref=buffer.at[me], send_sem=send.at[i], recv_sem=recv.at[i],
                 device_id=device, device_id_type=MESH))
             copies[-1].start()
+        return copies
+
+    def total_of(buffer, copies):
         for c in copies:
             c.wait_recv()
-        return functools.reduce(jnp.add, [buffer[i] for i in range(len(partners) + 1)]), copies
-
-    part, first = exchange(sums, partial, x * 4 + y, [in_plane(*p) for p in plane], sum_send, sum_recv)
-    whole, second = exchange(total, part, z * 4 + grp, [over(*a) for a in across], tot_send, tot_recv)
+        return functools.reduce(jnp.add, [buffer[i] for i in range(len(copies) + 1)])
+
+    first = exchange(sums, partial, x * 4 + y, [in_plane(*p) for p in plane], sum_send, sum_recv)
+    best_ref[...] = best.reshape(rows)
+    for slot in HELD:
+        back_copy(slot).wait_send()
+    part = total_of(sums, first)
+    second = exchange(total, part, z * 4 + grp, [over(*a) for a in same_core + other_core], tot_send, tot_recv)
+    for c in first:
+        c.wait_send()
+    whole = total_of(total, second)
     mean = whole / jnp.concatenate([whole[:, 64:], whole[:, :64]], axis=1)
     mean_ref[...] = mean.reshape(128)[:mean_ref.shape[0]]
-
-    for slot in LINKS:
-        for q in range(pieces):
-            copy(slot, q).wait_send()
-        ids_copy(slot).wait_send()
-    for slot in HELD:
-        back_copy(slot).wait_send()
-    for c in first + second:
+    for c in second:
         c.wait_send()
 
 
@@ -289,8 +334,9 @@
             dma((6,)), dma((6,)),
             dma((15,)), dma((15,)),
             dma((7,)), dma((7,)),
+            pltpu.SemaphoreType.REGULAR,
         ],
-        compiler_params=pltpu.CompilerParams(collective_id=0, has_side_effects=True, vmem_limit_bytes=63 * 2**20),
+        compiler_params=pltpu.CompilerParams(collective_id=0, has_side_effects=True, vmem_limit_bytes=107 * 2**19),
     )(embeddings, cluster_ids)
 
 

time: 59.7 us -> 56 us (0.938)
  Pallas kernels: 57.1 us -> 53.4 us
    pallas_call x1, Pallas kernels: 57.1 us -> 53.4 us  [per_device(): pl.pallas_call(kernel, out_shape=(jax.ShapeDtypeStruct((rows,), jnp.float...]
where the time goes in v2:
time: 56 us; the launch traced here: 55.9 us
  Pallas kernels  53.4 us (95%)
  local copies, waits for them, and re-layouts  1.79 us (3%)
  between operations  0.65 us (1%)
    pallas_call x1, Pallas kernels, per_device(): pl.pallas_call(kernel, out_shape=(jax.ShapeDtypeStruct((rows,), jnp.float...  53.4 us
    unnamed x4, local copies, waits for them, and re-layouts  1.79 us

profile of v2, /device:TPU:1, one launch (start us, length us, event | category | flops | bytes accessed | tf_op | source)
XLA Modules:
  0.0 55.9 jit_solution(3085423179793521653)
XLA Ops:
  0.6 0.0 copy-start
  0.6 0.7 %copy-done = s32[768]{0:T(1024)S(1)} copy-done((s32[768]{0:T(1024)S(1)}, s32[768]{0:T(1024)}, u32[]{:S(2)}) %copy-start) | copy-done | bytes 3096
  1.3 53.4 %shard_map.41 = (f32[768]{0:T(1024)S(1)}, f32[12]{0:T(128)S(1)}) custom-call(bf16[768,512]{1,0:T(8,128)(2,1)} %x_hbm.1, s32[768]{0:T(1024)S(1)} %copy-done), custom_call_target="tpu_custom_call" | custom-call | tf_op jit(solution)/shard_map/pallas_call | solution.py:312
  54.7 0.6 %copy.6 = f32[768]{0:T(1024)} copy(f32[768]{0:T(1024)S(1)} %get-tuple-element.4) | data formatting | bytes 6144
  55.3 0.5 copy.7
Async XLA Ops:
  0.6 0.7 %copy-start = (s32[768]{0:T(1024)S(1)}, s32[768]{0:T(1024)}, u32[]{:S(2)}) copy-start(s32[768]{0:T(1024)} %ids_hbm.1) | copy-start | bytes 9220

commit v3 on v2

--- a/solution.py
+++ b/solution.py
@@ -24,48 +24,55 @@
     F: (RELAY, (0, 1, 0)),
     G: (RELAY, (1, 0, 0)),
 }
+LATE_F = 0
+
+
+def link(slot, q, pieces):
+    if slot == F and q >= pieces - LATE_F:
+        return A, (0, 0, 1)
+    return LINKS[slot]
+
+
 WHOLE = ((B, OWN), (C, OWN), (C, B), (A, C), (F, OWN), (F, B), (F, C), (G, OWN), (G, B), (G, C), (G, F), (E, OWN))
 HALVED = ((A, B), (A, F), (A, G), (E, B), (E, F), (E, G), (E, A))
 PASS, SEND, TILE_OF = range(3)
 ORDER = (
     (PASS, B, 0),
+    (TILE_OF, A, 0),
+    (PASS, RELAY, 0),
+    (PASS, RELAY, 1),
     (PASS, B, 1),
-    (TILE_OF, A, 0),
+    (PASS, B, 2),
+    (PASS, B, 3),
     (TILE_OF, B, 0),
-    (PASS, RELAY, 0),
-    (PASS, B, 2),
+    (PASS, RELAY, 2),
     (TILE_OF, A, 1),
-    (PASS, RELAY, 1),
-    (PASS, B, 3),
     (PASS, C, 0),
+    (PASS, RELAY, 3),
+    (PASS, B, 4),
+    (PASS, B, 5),
+    (TILE_OF, B, 2),
     (TILE_OF, B, 1),
-    (PASS, RELAY, 2),
+    (TILE_OF, C, 0),
+    (PASS, RELAY, 4),
     (PASS, C, 1),
-    (TILE_OF, C, 0),
-    (PASS, B, 4),
+    (PASS, C, 2),
+    (TILE_OF, A, 2),
+    (TILE_OF, F, 0),
+    (TILE_OF, C, 1),
     (TILE_OF, G, 0),
-    (PASS, RELAY, 3),
-    (TILE_OF, F, 0),
-    (PASS, C, 2),
-    (PASS, B, 5),
-    (PASS, RELAY, 4),
-    (TILE_OF, B, 2),
     (PASS, C, 3),
-    (TILE_OF, C, 1),
+    (PASS, C, 4),
     (PASS, RELAY, 5),
-    (SEND, A, 4),
-    (SEND, A, 5),
+    (PASS, C, 5),
+    (TILE_OF, F, 1),
+    (TILE_OF, C, 2),
     (TILE_OF, E, 0),
     (TILE_OF, G, 1),
-    (PASS, C, 4),
-    (TILE_OF, F, 1),
-    (PASS, C, 5),
-    (TILE_OF, C, 2),
     (TILE_OF, E, 1),
     (TILE_OF, F, 2),
+    (TILE_OF, E, 2),
     (TILE_OF, G, 2),
-    (TILE_OF, A, 2),
-    (TILE_OF, E, 2),
 )
 
 
@@ -111,7 +118,7 @@
         pl.semaphore_signal(barrier, inc=1, device_id=device, device_id_type=MESH)
 
     def copy(slot, q):
-        source, step = LINKS[slot]
+        source, step = link(slot, q, pieces)
         window = pl.ds(q * PIECE, PIECE)
         return pltpu.make_async_remote_copy(
             src_ref=held.at[source, window], dst_ref=held.at[slot, window], send_sem=send_sem.at[slot - 1, q],
@@ -201,13 +208,14 @@
 
     def pass_on(slot, q):
         wait(slot, q)
-        onward = [to for to, (source, _) in LINKS.items() if source == slot]
-        for to in onward:
-            copy(to, q).start()
+        for to in LINKS:
+            if link(to, q, pieces)[0] == slot:
+                copy(to, q).start()
         if q == 0:
             wait_ids(slot)
-            for to in onward:
-                ids_copy(to).start()
+            for to, (source, _) in LINKS.items():
+                if source == slot:
+                    ids_copy(to).start()
 
     load_ids.wait()
     ids = ids_ref[...].reshape(1, rows)
@@ -336,7 +344,7 @@
             dma((7,)), dma((7,)),
             pltpu.SemaphoreType.REGULAR,
         ],
-        compiler_params=pltpu.CompilerParams(collective_id=0, has_side_effects=True, vmem_limit_bytes=107 * 2**19),
+        compiler_params=pltpu.CompilerParams(collective_id=0, has_side_effects=True, vmem_limit_bytes=863 * 2**16 - 2**13),
     )(embeddings, cluster_ids)
 
 

time: 56 us -> 54.9 us (0.980)
  local copies, waits for them, and re-layouts: 1.79 us -> 1.11 us
    unnamed x4 -> x2, local copies, waits for them, and re-layouts: 1.79 us -> 1.11 us
where the time goes in v3:
time: 54.9 us; the launch traced here: 54.8 us
  Pallas kernels  53.1 us (97%)
  local copies, waits for them, and re-layouts  1.11 us (2%)
  between operations  0.64 us (1%)
    pallas_call x1, Pallas kernels, per_device(): pl.pallas_call(kernel, out_shape=(jax.ShapeDtypeStruct((rows,), jnp.float...  53.1 us
    unnamed x2, local copies, waits for them, and re-layouts  1.11 us

profile of v3, /device:TPU:1, one launch (start us, length us, event | category | flops | bytes accessed | tf_op | source)
XLA Modules:
  0.0 54.8 jit_solution(6752248590413502876)
XLA Ops:
  0.6 53.1 %shard_map.41 = (f32[768]{0:T(1024)S(1)}, f32[12]{0:T(128)S(1)}) custom-call(bf16[768,512]{1,0:T(8,128)(2,1)} %x_hbm.1, s32[768]{0:T(1024)} %ids_hbm.1), custom_call_target="tpu_custom_call" | custom-call | tf_op jit(solution)/shard_map/pallas_call | solution.py:320
  53.7 0.6 %copy.6 = f32[768]{0:T(1024)} copy(f32[768]{0:T(1024)S(1)} %get-tuple-element.4) | data formatting | bytes 6144
  54.3 0.5 copy.7

commit v4 on v2

--- a/solution.py
+++ b/solution.py
@@ -26,46 +26,49 @@
 }
 WHOLE = ((B, OWN), (C, OWN), (C, B), (A, C), (F, OWN), (F, B), (F, C), (G, OWN), (G, B), (G, C), (G, F), (E, OWN))
 HALVED = ((A, B), (A, F), (A, G), (E, B), (E, F), (E, G), (E, A))
-PASS, SEND, TILE_OF = range(3)
+PASS, SEND, TILE_OF, CUT = range(4)
 ORDER = (
+    (PASS, RELAY, 0),
+    (TILE_OF, B, 0),
     (PASS, B, 0),
+    (TILE_OF, B, 1),
     (PASS, B, 1),
-    (TILE_OF, A, 0),
-    (TILE_OF, B, 0),
-    (PASS, RELAY, 0),
     (PASS, B, 2),
-    (TILE_OF, A, 1),
     (PASS, RELAY, 1),
+    (PASS, RELAY, 2),
     (PASS, B, 3),
     (PASS, C, 0),
-    (TILE_OF, B, 1),
-    (PASS, RELAY, 2),
     (PASS, C, 1),
+    (PASS, B, 4),
+    (TILE_OF, A, 0),
+    (PASS, RELAY, 3),
+    (TILE_OF, G, 0),
+    (TILE_OF, F, 0),
+    (PASS, B, 5),
+    (PASS, C, 2),
+    (PASS, RELAY, 4),
+    (TILE_OF, C, 1),
+    (TILE_OF, A, 1),
+    (TILE_OF, B, 2),
     (TILE_OF, C, 0),
-    (PASS, B, 4),
-    (TILE_OF, G, 0),
-    (PASS, RELAY, 3),
-    (TILE_OF, F, 0),
-    (PASS, C, 2),
-    (PASS, B, 5),
-    (PASS, RELAY, 4),
-    (TILE_OF, B, 2),
+    (PASS, RELAY, 5),
     (PASS, C, 3),
-    (TILE_OF, C, 1),
-    (PASS, RELAY, 5),
+    (TILE_OF, F, 1),
+    (TILE_OF, E, 0),
     (SEND, A, 4),
     (SEND, A, 5),
-    (TILE_OF, E, 0),
+    (PASS, C, 4),
+    (PASS, C, 5),
     (TILE_OF, G, 1),
-    (PASS, C, 4),
-    (TILE_OF, F, 1),
-    (PASS, C, 5),
     (TILE_OF, C, 2),
+    (CUT, OWN, 0),
     (TILE_OF, E, 1),
+    (CUT, OWN, 0),
+    (TILE_OF, G, 2),
     (TILE_OF, F, 2),
-    (TILE_OF, G, 2),
+    (CUT, OWN, 0),
+    (TILE_OF, E, 2),
     (TILE_OF, A, 2),
-    (TILE_OF, E, 2),
 )
 
 
@@ -105,28 +108,33 @@
     same_core = [(1, 0, 0), (0, 1, 0), (1, 1, 0)]
     other_core = [(1, 0, 1), (0, 1, 1), (1, 1, 1), (0, 0, 1)]
 
+    next_device = {slot: times(step) for slot, (_, step) in LINKS.items()}
+    owner = {slot: times(step) for slot, step in HELD.items()}
+    plane_devices = [in_plane(*p) for p in plane]
+    column_devices = [over(*a) for a in same_core + other_core]
+
     barrier = pltpu.get_barrier_semaphore()
     greeted = [over(*a) for a in same_core] + [in_plane(*p) for p in ((0, 1), (0, 3), (1, 0), (3, 0))] + [over(0, 0, 1)]
     for device in greeted:
         pl.semaphore_signal(barrier, inc=1, device_id=device, device_id_type=MESH)
 
     def copy(slot, q):
-        source, step = LINKS[slot]
+        source = LINKS[slot][0]
         window = pl.ds(q * PIECE, PIECE)
         return pltpu.make_async_remote_copy(
             src_ref=held.at[source, window], dst_ref=held.at[slot, window], send_sem=send_sem.at[slot - 1, q],
-            recv_sem=recv_sem.at[slot - 1, q], device_id=times(step), device_id_type=MESH)
+            recv_sem=recv_sem.at[slot - 1, q], device_id=next_device[slot], device_id_type=MESH)
 
     def ids_copy(slot):
-        source, step = LINKS[slot]
+        source = LINKS[slot][0]
         return pltpu.make_async_remote_copy(
             src_ref=counts.at[source], dst_ref=counts.at[slot], send_sem=ids_send.at[slot - 1],
-            recv_sem=ids_recv.at[slot - 1], device_id=times(step), device_id_type=MESH)
+            recv_sem=ids_recv.at[slot - 1], device_id=next_device[slot], device_id_type=MESH)
 
     def back_copy(slot):
         return pltpu.make_async_remote_copy(
             src_ref=back.at[slot], dst_ref=got.at[slot], send_sem=back_send.at[slot - 1],
-            recv_sem=back_recv.at[slot - 1], device_id=times(HELD[slot]), device_id_type=MESH)
+            recv_sem=back_recv.at[slot - 1], device_id=owner[slot], device_id_type=MESH)
 
     def normalise(q):
         load(q).wait()
@@ -172,6 +180,11 @@
             if slot != RELAY:
                 fill_ids(slot)
 
+    def wait_tile(s, q):
+        for p in range(q * TILE // PIECE, (q + 1) * TILE // PIECE):
+            wait(s, p)
+        wait_ids(s)
+
     def wanted(s, q, j, r):
         if (s, j) in WHOLE or (j, s) in WHOLE:
             return True
@@ -184,9 +197,7 @@
             if q + 1 < tiles:
                 product(OWN, (q + 1) * TILE, rows - (q + 1) * TILE, OWN, q)
             return
-        for p in range(q * TILE // PIECE, (q + 1) * TILE // PIECE):
-            wait(s, p)
-        wait_ids(s)
+        wait_tile(s, q)
         for j in (OWN, *HELD):
             if j == s:
                 continue
@@ -242,12 +253,16 @@
     here = lane == base + sublane
     numbers = jnp.sum(jnp.where((lane == base + sublane + 64) & (sublane < CL_GRP), number, 0.0), axis=0, keepdims=True)
 
-    for action, slot, q in ORDER:
+    for i, (action, slot, q) in enumerate(ORDER):
         if action == PASS:
             pass_on(slot, q)
         elif action == SEND:
             copy(slot, q).start()
-        else:
+        elif action == TILE_OF:
+            for group_action, s, t in ORDER[i:]:
+                if group_action != TILE_OF:
+                    break
+                wait_tile(s, t)
             multiply(slot, q)
 
     def finish(slot):
@@ -288,12 +303,12 @@
             c.wait_recv()
         return functools.reduce(jnp.add, [buffer[i] for i in range(len(copies) + 1)])
 
-    first = exchange(sums, partial, x * 4 + y, [in_plane(*p) for p in plane], sum_send, sum_recv)
+    first = exchange(sums, partial, x * 4 + y, plane_devices, sum_send, sum_recv)
     best_ref[...] = best.reshape(rows)
     for slot in HELD:
         back_copy(slot).wait_send()
     part = total_of(sums, first)
-    second = exchange(total, part, z * 4 + grp, [over(*a) for a in same_core + other_core], tot_send, tot_recv)
+    second = exchange(total, part, z * 4 + grp, column_devices, tot_send, tot_recv)
     for c in first:
         c.wait_send()
     whole = total_of(total, second)
@@ -336,7 +351,7 @@
             dma((7,)), dma((7,)),
             pltpu.SemaphoreType.REGULAR,
         ],
-        compiler_params=pltpu.CompilerParams(collective_id=0, has_side_effects=True, vmem_limit_bytes=107 * 2**19),
+        compiler_params=pltpu.CompilerParams(collective_id=0, has_side_effects=True, vmem_limit_bytes=863 * 2**16 - 2**13),
     )(embeddings, cluster_ids)
 
 

time: 56 us -> 53.7 us (0.959)
  Pallas kernels: 53.4 us -> 51.8 us
  local copies, waits for them, and re-layouts: 1.79 us -> 1.11 us
    pallas_call x1, Pallas kernels: 53.4 us -> 51.8 us  [per_device(): pl.pallas_call(kernel, out_shape=(jax.ShapeDtypeStruct((rows,), jnp.float...]
    unnamed x4 -> x2, local copies, waits for them, and re-layouts: 1.79 us -> 1.11 us
where the time goes in v4:
time: 53.7 us; the launch traced here: 53.6 us
  Pallas kernels  51.8 us (96%)
  local copies, waits for them, and re-layouts  1.11 us (2%)
  between operations  0.64 us (1%)
    pallas_call x1, Pallas kernels, per_device(): pl.pallas_call(kernel, out_shape=(jax.ShapeDtypeStruct((rows,), jnp.float...  51.8 us
    unnamed x2, local copies, waits for them, and re-layouts  1.11 us

profile of v4, /device:TPU:1, one launch (start us, length us, event | category | flops | bytes accessed | tf_op | source)
XLA Modules:
  0.0 53.6 jit_solution(18348922211643994461)
XLA Ops:
  0.6 51.8 %shard_map.41 = (f32[768]{0:T(1024)S(1)}, f32[12]{0:T(128)S(1)}) custom-call(bf16[768,512]{1,0:T(8,128)(2,1)} %x_hbm.1, s32[768]{0:T(1024)} %ids_hbm.1), custom_call_target="tpu_custom_call" | custom-call | tf_op jit(solution)/shard_map/pallas_call | solution.py:327
  52.5 0.6 %copy.6 = f32[768]{0:T(1024)} copy(f32[768]{0:T(1024)S(1)} %get-tuple-element.4) | data formatting | bytes 6144
  53.1 0.5 copy.7

commit v5 on v4

--- a/solution.py
+++ b/solution.py
@@ -52,11 +52,11 @@
     (TILE_OF, B, 2),
     (TILE_OF, C, 0),
     (PASS, RELAY, 5),
+    (SEND, A, 4),
+    (SEND, A, 5),
     (PASS, C, 3),
     (TILE_OF, F, 1),
     (TILE_OF, E, 0),
-    (SEND, A, 4),
-    (SEND, A, 5),
     (PASS, C, 4),
     (PASS, C, 5),
     (TILE_OF, G, 1),

time: 53.7 us -> 53.7 us (level)
  no operation moved by 1% of the time
where the time goes in v5:
time: 53.7 us; the launch traced here: 53.6 us
  Pallas kernels  51.8 us (96%)
  local copies, waits for them, and re-layouts  1.11 us (2%)
  between operations  0.64 us (1%)
    pallas_call x1, Pallas kernels, per_device(): pl.pallas_call(kernel, out_shape=(jax.ShapeDtypeStruct((rows,), jnp.float...  51.8 us
    unnamed x2, local copies, waits for them, and re-layouts  1.11 us

profile of v5, /device:TPU:1, one launch (start us, length us, event | category | flops | bytes accessed | tf_op | source)
XLA Modules:
  0.0 53.6 jit_solution(7414503462748161311)
XLA Ops:
  0.6 51.8 %shard_map.41 = (f32[768]{0:T(1024)S(1)}, f32[12]{0:T(128)S(1)}) custom-call(bf16[768,512]{1,0:T(8,128)(2,1)} %x_hbm.1, s32[768]{0:T(1024)} %ids_hbm.1), custom_call_target="tpu_custom_call" | custom-call | tf_op jit(solution)/shard_map/pallas_call | solution.py:327
  52.5 0.6 %copy.6 = f32[768]{0:T(1024)} copy(f32[768]{0:T(1024)S(1)} %get-tuple-element.4) | data formatting | bytes 6144
  53.1 0.5 copy.7
